TPU v7x, 32 devices: a whole 2x2x4 slice. The times are simulated.
32 devices in a mesh: energy: 16 (over z, y, core), section: 2 (over x).
Axes of the slice: x: 2, y: 2, z: 4, core: 2. Of those that a mesh axis runs over, the one named last changes fastest.
Arguments:
- green_prev: float32 [32, 2, 2, 256, 256], P('energy', 'section'), may hold values from -0.2 to 0.2
- slab_ham: float32 [2, 2, 256, 256], P('section'), may hold values from -0.046875 to 0.046875
- onsite: float32 [2, 256], P('section'), may hold values from -1.5 to 1.5
- hop: float32 [2, 2, 256, 256], P('section'), may hold values from -0.94 to 0.94
- mode_strength: float32 [6], replicated, may hold values from 0.03 to 0.15
- phonon_shift: int32 [6], replicated, may hold values from 1 to 2, as said below
Outputs:
- green_diag: float32 [32, 2, 2, 256, 256], P('energy', 'section')
Inputs may be any that keep to these rules, and one draw needn't show every extreme that they name: `phonon_shift`: every shift is at least 1 and at most 2; some mode reaches 2.
All inputs are finite; a program needn't handle non-finite values.
Results may differ from a plain program's by a relative error of at most 0.00012.
Values sent between devices are 32-bit elements; how exact they have to be, the bound alone decides.
A program may use at most 64 MiB of HBM per device.

v0:
```python
from functools import partial

import jax
import jax.numpy as jnp
from jax import lax
from jax.sharding import PartitionSpec as P

ETA = 1.0
LEAD = 0.5


def extended(block, sides, width):
    for axis, dim in sides:
        count = lax.axis_size(axis)
        forward = [(i, i + 1) for i in range(count - 1)]
        backward = [(target, source) for source, target in forward]
        low = lax.ppermute(
            lax.slice_in_dim(block, block.shape[dim] - width, None, axis=dim), axis, forward
        )
        high = lax.ppermute(lax.slice_in_dim(block, 0, width, axis=dim), axis, backward)
        block = jnp.concatenate([low, block, high], axis=dim)
    return block


def shifted(array, axis, by):
    count = lax.axis_size(axis)
    pairs = [(i, i + by) for i in range(count) if 0 <= i + by < count]
    return lax.ppermute(array, axis, pairs)


def cmul(left_op, right_op):
    matmul = partial(jnp.matmul, precision=lax.Precision.HIGHEST)
    lre, lim = (left_op[..., 0, :, :], left_op[..., 1, :, :])
    rre, rim = (right_op[..., 0, :, :], right_op[..., 1, :, :])
    return jnp.stack(
        [matmul(lre, rre) - matmul(lim, rim), matmul(lre, rim) + matmul(lim, rre)], axis=-3
    )


def adjoint(block):
    return jnp.stack(
        [jnp.swapaxes(block[..., 0, :, :], -1, -2), -jnp.swapaxes(block[..., 1, :, :], -1, -2)],
        axis=-3,
    )


def left_connected(left, energies, sigma, ham, site, link, eye):
    couple = cmul(cmul(adjoint(link), left), link)
    real_part = energies[:, None, None] * eye[None]
    imag_part = ETA * eye[None]
    matrix = jnp.stack([real_part, imag_part], axis=1) - ham[None] - sigma - couple
    offset = energies[:, None] - site[None, :]
    denom = offset * offset + ETA * ETA
    guess = jnp.stack(
        [eye[None] * (offset / denom)[:, None, :], eye[None] * (-ETA / denom)[:, None, :]], axis=1
    )
    for sweep_step in range(2):
        guess = 2.0 * guess - cmul(guess, cmul(matrix, guess))
    return guess


def full_and_message(left, message, link):
    full = left + cmul(left, cmul(message, left))
    return (full, cmul(cmul(link, full), adjoint(link)))


def body(green_prev, slab_ham, onsite, hop, mode_strength, phonon_shift):
    ne_dev = green_prev.shape[0]
    norb = green_prev.shape[3]
    eye = jnp.eye(norb, dtype=jnp.float32)
    padded = extended(green_prev, (("energy", 0),), ne_dev)
    sigma = jnp.zeros((ne_dev, 2, norb, norb), jnp.float32)
    for mode in range(mode_strength.shape[0]):
        shift = phonon_shift[mode]
        lower = lax.dynamic_slice_in_dim(padded, ne_dev - shift, ne_dev, 0)
        upper = lax.dynamic_slice_in_dim(padded, ne_dev + shift, ne_dev, 0)
        sigma = sigma + mode_strength[mode] * (lower[:, 0] + upper[:, 0])
    count = ne_dev * lax.axis_size("energy")
    first = lax.axis_index("energy") * ne_dev
    energies = (
        -1.5
        + 3.0 * ((first + jnp.arange(ne_dev, dtype=jnp.int32)).astype(jnp.float32) + 0.5) / count
    )
    site = onsite[0]
    block = slab_ham[0]
    herm = 0.5 * (block + adjoint(block))
    ham = jnp.stack([herm[0] + eye * site[None, :], herm[1]])
    link = hop[0]
    section = lax.axis_index("section")
    nsec = lax.axis_size("section")
    zero_block = jnp.zeros((norb, norb), jnp.float32)
    lead_one = jnp.stack([zero_block, -LEAD * eye])[None]
    empty_one = jnp.zeros((1, 2, norb, norb), jnp.float32)
    empty_all = jnp.zeros((ne_dev, 2, norb, norb), jnp.float32)

    def forward_turn(turn, carry):
        received, stored = carry
        slot = turn - section
        active = (slot >= 0) & (slot < ne_dev)
        pick = jnp.clip(slot, 0, ne_dev - 1)
        left = jnp.where(section == 0, lead_one, received)
        energy_one = lax.dynamic_slice_in_dim(energies, pick, 1, 0)
        sigma_one = lax.dynamic_slice_in_dim(sigma, pick, 1, 0)
        result = lax.cond(
            active,
            lambda: left_connected(left, energy_one, sigma_one, ham, site, link, eye),
            lambda: empty_one,
        )
        stored = jnp.where(active, lax.dynamic_update_slice_in_dim(stored, result, pick, 0), stored)
        received = shifted(result, "section", 1)
        return (received, stored)

    unused, lefts = lax.fori_loop(0, nsec + ne_dev - 1, forward_turn, (empty_one, empty_all))

    def backward_turn(turn, carry):
        received, stored = carry
        slot = turn - (nsec - 1 - section)
        active = (slot >= 0) & (slot < ne_dev)
        pick = jnp.clip(slot, 0, ne_dev - 1)
        message = jnp.where(section == nsec - 1, empty_one, received)
        left_one = lax.dynamic_slice_in_dim(lefts, pick, 1, 0)
        full, sent = lax.cond(
            active,
            lambda: full_and_message(left_one, message, link),
            lambda: (empty_one, empty_one),
        )
        stored = jnp.where(active, lax.dynamic_update_slice_in_dim(stored, full, pick, 0), stored)
        received = shifted(sent, "section", -1)
        return (received, stored)

    unused, fulls = lax.fori_loop(0, nsec + ne_dev - 1, backward_turn, (empty_one, empty_all))
    return fulls[:, None]


def solution(mesh):
    return jax.shard_map(
        body,
        mesh=mesh,
        in_specs=(
            P("energy", "section", None, None, None),
            P("section", None, None, None),
            P("section", None),
            P("section", None, None, None),
            P(),
            P(),
        ),
        out_specs=P("energy", "section", None, None, None),
        check_vma=False,
    )
```

profile of v0, /device:TPU:0, one launch (start us, length us, event | category | flops | bytes accessed | tf_op | source)
XLA Modules:
  0.0 202.6 jit_solution(2470959654201098641)
XLA Ops:
  0.0 3.5 %collective-permute-start.2 = (f32[2,1,2,256,256]{4,3,2,0,1:T(8,128)}, f32[2,1,2,256,256]{4,3,2,0,1:T(8,128)}, u32[]{:S(2)}, u32[]{:S(2)}) collective-permute-start(f32[2,1,2,256,256]{4,3,2,0,1:T(8,128)} %bitcast.228), channel_id=1, source_target_pairs={{0,2},{2,4},{4,6},{6,8},{8,10},{10,12},{12,14},{14,16},{16,18},{18... | collective-permute-start | bytes 3145736 | tf_op jit(solution)/shard_map/ppermute | solution.py:17
  4.8 1.6 fusion.98
  22.8 1.6 fusion.97
  25.4 1.7 pad_maximum_fusion.1
  27.1 5.8 %add_bitcast_fusion = f32[2,2,256,256]{3,2,1,0:T(8,128)} fusion(f32[6,1,2,256,256]{4,3,2,0,1:T(8,128)S(1)} %pad_maximum_fusion.1, s32[]{:T(128)S(6)} %select_n.132, s32[]{:T(128)S(6)} %select_n.131, s32[]{:T(128)S(6)} %select_n.130, s32[]{:T(128)S(6)} %select_n.129, s32[]{:T(128)S(6)} %select_n.128, s32[]{:T(128)S(6)} %select_n.127, s32[]{:T(128)S(6)} %select_n.126, ...), kind=kLoop, calls=%fused_computation.143 | loop fusion | flops 4456448 | bytes 13631560 | tf_op jit(solution)/shard_map/add | solution.py:77
  33.0 84.2 %while.36 = (s32[]{:T(128)}, f32[1,2,256,256]{3,2,1,0:T(8,128)S(1)}, f32[2,2,256,256]{3,2,1,0:T(8,128)S(1)}, s32[]{:T(128)}, f32[1,256]{1,0:T(1,128)S(1)}, /*ind...) while((s32[]{:T(128)}, ...), condition=%wide.region_3.4_spmd.clone.clone, body=%wide.region_0.3_spmd.clone.clone.sunk | while | flops 4835968000 | bytes 41694668 | solution.py:113
  33.3 13.6 %conditional.7 = (f32[1,2,256,256]{3,2,1,0:T(8,128)S(1)}) conditional(s32[]{:T(128)} %convert_element_type.50, () %tuple.124, (f32[2]{0:T(128)S(1)}, s32[]{:T(128)}, f32[1,256]{1,0:T(1,128)S(1)}, f32[256,256]{1,0:T(8,128)S(1)}, f32[256,256]{1,0:T(8,128)S(1)}, /*index=5*/f32[256,256]{1,0:T(8,128)S(1)}, f32[256,256]{1,0:T(8,128)S(1)}, ...), branch_computations={%region_1.1_spmd, %region_2.2_spmd.clone} | conditional | flops 4835705856 | bytes 37762152 | solution.py:104
  46.9 1.3 collective-permute-start.1
  48.3 9.7 %collective-permute-done.1 = f32[1,2,256,256]{3,2,1,0:T(8,128)S(1)} collective-permute-done((f32[1,2,256,256]{3,2,1,0:T(8,128)S(1)}, f32[1,2,256,256]{3,2,1,0:T(8,128)S(1)}, u32[]{:S(2)}, u32[]{:S(2)}) %collective-permute-start.1) | collective-permute-done | bytes 524320 | tf_op jit(solution)/shard_map/while/body/eval_jaxpr/ppermute | solution.py:28
  58.1 13.6 %conditional.7 = (f32[1,2,256,256]{3,2,1,0:T(8,128)S(1)}) conditional(s32[]{:T(128)} %convert_element_type.50, () %tuple.124, (f32[2]{0:T(128)S(1)}, s32[]{:T(128)}, f32[1,256]{1,0:T(1,128)S(1)}, f32[256,256]{1,0:T(8,128)S(1)}, f32[256,256]{1,0:T(8,128)S(1)}, /*index=5*/f32[256,256]{1,0:T(8,128)S(1)}, f32[256,256]{1,0:T(8,128)S(1)}, ...), branch_computations={%region_1.1_spmd, %region_2.2_spmd.clone} | conditional | flops 4835705856 | bytes 37762152 | solution.py:104
  71.7 4.4 %collective-permute-start.1 = (f32[1,2,256,256]{3,2,1,0:T(8,128)S(1)}, f32[1,2,256,256]{3,2,1,0:T(8,128)S(1)}, u32[]{:S(2)}, u32[]{:S(2)}) collective-permute-start(f32[1,2,256,256]{3,2,1,0:T(8,128)S(1)} %get-tuple-element.878), channel_id=1, source_target_pairs={{0,1},{2,3},{4,5},{6,7},{8,9},{10,11},{12,13},{14,15},{16,17},{18,... | collective-permute-start | bytes 1572872 | tf_op jit(solution)/shard_map/while/body/eval_jaxpr/ppermute | solution.py:28
  76.2 10.9 %collective-permute-done.1 = f32[1,2,256,256]{3,2,1,0:T(8,128)S(1)} collective-permute-done((f32[1,2,256,256]{3,2,1,0:T(8,128)S(1)}, f32[1,2,256,256]{3,2,1,0:T(8,128)S(1)}, u32[]{:S(2)}, u32[]{:S(2)}) %collective-permute-start.1) | collective-permute-done | bytes 524320 | tf_op jit(solution)/shard_map/while/body/eval_jaxpr/ppermute | solution.py:28
  87.2 17.9 %collective-permute-start.1 = (f32[1,2,256,256]{3,2,1,0:T(8,128)S(1)}, f32[1,2,256,256]{3,2,1,0:T(8,128)S(1)}, u32[]{:S(2)}, u32[]{:S(2)}) collective-permute-start(f32[1,2,256,256]{3,2,1,0:T(8,128)S(1)} %get-tuple-element.878), channel_id=1, source_target_pairs={{0,1},{2,3},{4,5},{6,7},{8,9},{10,11},{12,13},{14,15},{16,17},{18,... | collective-permute-start | bytes 1572872 | tf_op jit(solution)/shard_map/while/body/eval_jaxpr/ppermute | solution.py:28
  105.3 12.0 %collective-permute-done.1 = f32[1,2,256,256]{3,2,1,0:T(8,128)S(1)} collective-permute-done((f32[1,2,256,256]{3,2,1,0:T(8,128)S(1)}, f32[1,2,256,256]{3,2,1,0:T(8,128)S(1)}, u32[]{:S(2)}, u32[]{:S(2)}) %collective-permute-start.1) | collective-permute-done | bytes 524320 | tf_op jit(solution)/shard_map/while/body/eval_jaxpr/ppermute | solution.py:28
  118.4 84.2 %while.35 = (s32[]{:T(128)}, f32[1,2,256,256]{3,2,1,0:T(8,128)S(1)}, f32[2,2,256,256]{3,2,1,0:T(8,128)}, s32[]{:T(128)}, f32[2,2,256,256]{3,2,1,0:T(8,128)S(1)},...) while((s32[]{:T(128)}, f32[1,2,256,256]{3,2,1,0:T(8,128)S(1)}, ...), condition=%wide.region_7.8_spmd, body=%wide.region_4.7_spmd.sunk | while | flops 3222536192 | bytes 22020932 | solution.py:131
  119.5 1.3 collective-permute-start
  120.8 1.9 select_dynamic-update-slice_fusion.4
  122.7 24.6 %collective-permute-done = f32[1,2,256,256]{3,2,1,0:T(8,128)S(1)} collective-permute-done((f32[1,2,256,256]{3,2,1,0:T(8,128)S(1)}, f32[1,2,256,256]{3,2,1,0:T(8,128)S(1)}, u32[]{:S(2)}, u32[]{:S(2)}) %collective-permute-start) | collective-permute-done | bytes 524320 | tf_op jit(solution)/shard_map/while/body/eval_jaxpr/ppermute | solution.py:28
  147.3 12.7 %conditional.6 = (f32[1,2,256,256]{3,2,1,0:T(8,128)}, f32[1,2,256,256]{3,2,1,0:T(8,128)S(1)}) conditional(s32[]{:T(128)} %convert_element_type.47, () %tuple.121, (f32[2,2,256,256]{3,2,1,0:T(8,128)S(1)}, s32[]{:T(128)}, pred[]{:T(512)}, f32[1,2,256,256]{3,2,1,0:T(8,128)S(1)}, f32[2,256,256]{2,1,0:T(8,128)S(1)}) %tuple.122), branch_computations={%region_5.5_spmd, %region_6.6_spmd} | conditional | flops 3222405120 | bytes 18350160 | solution.py:122
  151.4 1.5 fusion.11
  152.9 1.5 convolution_add_fusion.1
  154.5 1.5 fusion.15
  156.0 1.5 convolution_subtract_fusion.1
  161.4 2.1 %select_dynamic-update-slice_fusion.4 = f32[2,2,256,256]{3,2,1,0:T(8,128)} fusion(f32[2,2,256,256]{3,2,1,0:T(8,128)} %get-tuple-element.860, s32[]{:T(128)} %min.22, f32[1,2,256,256]{3,2,1,0:T(8,128)} %get-tuple-element.790, pred[]{:T(512)S(6)} %and.23), kind=kLoop, calls=%fused_computation.54.clone.1 | loop fusion | flops 131072 | bytes 1573377 | tf_op jit(solution)/shard_map/while/body/eval_jaxpr/jit(_where)/select_n | solution.py:127
  163.4 12.0 %collective-permute-done = f32[1,2,256,256]{3,2,1,0:T(8,128)S(1)} collective-permute-done((f32[1,2,256,256]{3,2,1,0:T(8,128)S(1)}, f32[1,2,256,256]{3,2,1,0:T(8,128)S(1)}, u32[]{:S(2)}, u32[]{:S(2)}) %collective-permute-start) | collective-permute-done | bytes 524320 | tf_op jit(solution)/shard_map/while/body/eval_jaxpr/ppermute | solution.py:28
  175.4 12.7 %conditional.6 = (f32[1,2,256,256]{3,2,1,0:T(8,128)}, f32[1,2,256,256]{3,2,1,0:T(8,128)S(1)}) conditional(s32[]{:T(128)} %convert_element_type.47, () %tuple.121, (f32[2,2,256,256]{3,2,1,0:T(8,128)S(1)}, s32[]{:T(128)}, pred[]{:T(512)}, f32[1,2,256,256]{3,2,1,0:T(8,128)S(1)}, f32[2,256,256]{2,1,0:T(8,128)S(1)}) %tuple.122), branch_computations={%region_5.5_spmd, %region_6.6_spmd} | conditional | flops 3222405120 | bytes 18350160 | solution.py:122
  179.5 1.5 fusion.11
  181.0 1.5 convolution_add_fusion.1
  182.6 1.5 fusion.15
  184.1 1.5 convolution_subtract_fusion.1
  189.4 2.1 %select_dynamic-update-slice_fusion.4 = f32[2,2,256,256]{3,2,1,0:T(8,128)} fusion(f32[2,2,256,256]{3,2,1,0:T(8,128)} %get-tuple-element.860, s32[]{:T(128)} %min.22, f32[1,2,256,256]{3,2,1,0:T(8,128)} %get-tuple-element.790, pred[]{:T(512)S(6)} %and.23), kind=kLoop, calls=%fused_computation.54.clone.1 | loop fusion | flops 131072 | bytes 1573377 | tf_op jit(solution)/shard_map/while/body/eval_jaxpr/jit(_where)/select_n | solution.py:127
  191.5 11.1 %collective-permute-done = f32[1,2,256,256]{3,2,1,0:T(8,128)S(1)} collective-permute-done((f32[1,2,256,256]{3,2,1,0:T(8,128)S(1)}, f32[1,2,256,256]{3,2,1,0:T(8,128)S(1)}, u32[]{:S(2)}, u32[]{:S(2)}) %collective-permute-start) | collective-permute-done | bytes 524320 | tf_op jit(solution)/shard_map/while/body/eval_jaxpr/ppermute | solution.py:28
  (144 shorter events, 49.1 us)
Async XLA Ops:
  0.0 24.4 %copy-start.3 = (f32[1,2,256,256]{3,2,1,0:T(8,128)S(1)}, f32[1,2,256,256]{3,2,1,0:T(8,128)}, u32[]{:S(2)}) copy-start(f32[1,2,256,256]{3,2,1,0:T(8,128)} %param.15) | copy-start | bytes 1572868
  0.0 24.5 %copy-start.5 = (f32[1,256]{1,0:T(1,128)S(1)}, f32[1,256]{1,0:T(1,128)}, u32[]{:S(2)}) copy-start(f32[1,256]{1,0:T(1,128)} %param.16) | copy-start | bytes 3076
  0.0 25.4 %collective-permute-start.2 = (f32[2,1,2,256,256]{4,3,2,0,1:T(8,128)}, f32[2,1,2,256,256]{4,3,2,0,1:T(8,128)}, u32[]{:S(2)}, u32[]{:S(2)}) collective-permute-start(f32[2,1,2,256,256]{4,3,2,0,1:T(8,128)} %bitcast.228), channel_id=1, source_target_pairs={{0,2},{2,4},{4,6},{6,8},{8,10},{10,12},{12,14},{14,16},{16,18},{18... | collective-permute-start | bytes 3145736 | tf_op jit(solution)/shard_map/ppermute | solution.py:17
  3.5 21.9 %collective-permute-start.3 = (f32[2,1,2,256,256]{4,3,2,0,1:T(8,128)}, f32[2,1,2,256,256]{4,3,2,0,1:T(8,128)}, u32[]{:S(2)}, u32[]{:S(2)}) collective-permute-start(f32[2,1,2,256,256]{4,3,2,0,1:T(8,128)} %bitcast.229), channel_id=1, source_target_pairs={{2,0},{4,2},{6,4},{8,6},{10,8},{12,10},{14,12},{16,14},{18,16},{20... | collective-permute-start | bytes 3145736 | tf_op jit(solution)/shard_map/ppermute | solution.py:20
  22.4 3.0 %copy-start.4 = (f32[2,1,2,256,256]{4,3,2,1,0:T(8,128)S(1)}, f32[2,1,2,256,256]{4,3,2,1,0:T(8,128)}, u32[]{:S(2)}) copy-start(f32[2,1,2,256,256]{4,3,2,1,0:T(8,128)} %param.14) | copy-start | bytes 3145732
  27.1 5.9 %copy-start = (f32[1,2,256,256]{3,2,1,0:T(8,128)S(1)}, f32[1,2,256,256]{3,2,1,0:T(8,128)}, u32[]{:S(2)}) copy-start(f32[1,2,256,256]{3,2,1,0:T(8,128)} %param.17) | copy-start | bytes 1572868
  34.6 5.0 %copy-start.1 = (f32[2,256,256]{2,1,0:T(8,128)S(1)}, f32[2,256,256]{2,1,0:T(8,128)}, u32[]{:S(2)}) copy-start(f32[2,256,256]{2,1,0:T(8,128)} %get-tuple-element.612) | copy-start | bytes 1572868 | tf_op jit(solution)/shard_map/while/body/eval_jaxpr/cond
  34.6 5.0 %copy-start.2 = (f32[2,2,256,256]{3,2,1,0:T(8,128)S(1)}, f32[2,2,256,256]{3,2,1,0:T(8,128)}, u32[]{:S(2)}) copy-start(f32[2,2,256,256]{3,2,1,0:T(8,128)} %get-tuple-element.613) | copy-start | bytes 3145732 | tf_op jit(solution)/shard_map/while/body/eval_jaxpr/cond
  46.9 11.2 %collective-permute-start.1 = (f32[1,2,256,256]{3,2,1,0:T(8,128)S(1)}, f32[1,2,256,256]{3,2,1,0:T(8,128)S(1)}, u32[]{:S(2)}, u32[]{:S(2)}) collective-permute-start(f32[1,2,256,256]{3,2,1,0:T(8,128)S(1)} %get-tuple-element.878), channel_id=1, source_target_pairs={{0,1},{2,3},{4,5},{6,7},{8,9},{10,11},{12,13},{14,15},{16,17},{18,... | collective-permute-start | bytes 1572872 | tf_op jit(solution)/shard_map/while/body/eval_jaxpr/ppermute | solution.py:28
  59.4 5.0 %copy-start.1 = (f32[2,256,256]{2,1,0:T(8,128)S(1)}, f32[2,256,256]{2,1,0:T(8,128)}, u32[]{:S(2)}) copy-start(f32[2,256,256]{2,1,0:T(8,128)} %get-tuple-element.612) | copy-start | bytes 1572868 | tf_op jit(solution)/shard_map/while/body/eval_jaxpr/cond
  59.4 5.0 %copy-start.2 = (f32[2,2,256,256]{3,2,1,0:T(8,128)S(1)}, f32[2,2,256,256]{3,2,1,0:T(8,128)}, u32[]{:S(2)}) copy-start(f32[2,2,256,256]{3,2,1,0:T(8,128)} %get-tuple-element.613) | copy-start | bytes 3145732 | tf_op jit(solution)/shard_map/while/body/eval_jaxpr/cond
  71.7 15.4 %collective-permute-start.1 = (f32[1,2,256,256]{3,2,1,0:T(8,128)S(1)}, f32[1,2,256,256]{3,2,1,0:T(8,128)S(1)}, u32[]{:S(2)}, u32[]{:S(2)}) collective-permute-start(f32[1,2,256,256]{3,2,1,0:T(8,128)S(1)} %get-tuple-element.878), channel_id=1, source_target_pairs={{0,1},{2,3},{4,5},{6,7},{8,9},{10,11},{12,13},{14,15},{16,17},{18,... | collective-permute-start | bytes 1572872 | tf_op jit(solution)/shard_map/while/body/eval_jaxpr/ppermute | solution.py:28
  87.2 30.1 %collective-permute-start.1 = (f32[1,2,256,256]{3,2,1,0:T(8,128)S(1)}, f32[1,2,256,256]{3,2,1,0:T(8,128)S(1)}, u32[]{:S(2)}, u32[]{:S(2)}) collective-permute-start(f32[1,2,256,256]{3,2,1,0:T(8,128)S(1)} %get-tuple-element.878), channel_id=1, source_target_pairs={{0,1},{2,3},{4,5},{6,7},{8,9},{10,11},{12,13},{14,15},{16,17},{18,... | collective-permute-start | bytes 1572872 | tf_op jit(solution)/shard_map/while/body/eval_jaxpr/ppermute | solution.py:28
  119.5 27.8 %collective-permute-start = (f32[1,2,256,256]{3,2,1,0:T(8,128)S(1)}, f32[1,2,256,256]{3,2,1,0:T(8,128)S(1)}, u32[]{:S(2)}, u32[]{:S(2)}) collective-permute-start(f32[1,2,256,256]{3,2,1,0:T(8,128)S(1)} %get-tuple-element.789), channel_id=1, source_target_pairs={{1,0},{3,2},{5,4},{7,6},{9,8},{11,10},{13,12},{15,14},{17,16},{19,... | collective-permute-start | bytes 1572872 | tf_op jit(solution)/shard_map/while/body/eval_jaxpr/ppermute | solution.py:28
  160.1 15.3 %collective-permute-start = (f32[1,2,256,256]{3,2,1,0:T(8,128)S(1)}, f32[1,2,256,256]{3,2,1,0:T(8,128)S(1)}, u32[]{:S(2)}, u32[]{:S(2)}) collective-permute-start(f32[1,2,256,256]{3,2,1,0:T(8,128)S(1)} %get-tuple-element.789), channel_id=1, source_target_pairs={{1,0},{3,2},{5,4},{7,6},{9,8},{11,10},{13,12},{15,14},{17,16},{19,... | collective-permute-start | bytes 1572872 | tf_op jit(solution)/shard_map/while/body/eval_jaxpr/ppermute | solution.py:28
  188.1 14.4 %collective-permute-start = (f32[1,2,256,256]{3,2,1,0:T(8,128)S(1)}, f32[1,2,256,256]{3,2,1,0:T(8,128)S(1)}, u32[]{:S(2)}, u32[]{:S(2)}) collective-permute-start(f32[1,2,256,256]{3,2,1,0:T(8,128)S(1)} %get-tuple-element.789), channel_id=1, source_target_pairs={{1,0},{3,2},{5,4},{7,6},{9,8},{11,10},{13,12},{15,14},{17,16},{19,... | collective-permute-start | bytes 1572872 | tf_op jit(solution)/shard_map/while/body/eval_jaxpr/ppermute | solution.py:28
where the time goes:
time: 204 us; the launch traced here: 203 us
  waiting for transfers between devices  80.2 us (39%)
  matrix products  45.1 us (22%)
  starting transfers between devices  32.3 us (16%)
  other arithmetic  20.2 us (10%)
  between operations  15.2 us (7%)
  local copies, waits for them, and re-layouts  7.93 us (4%)
    ppermute x6, waiting for transfers between devices, shifted(): return lax.ppermute(array, axis, pairs)  80.2 us
    ppermute x6, starting transfers between devices, shifted(): return lax.ppermute(array, axis, pairs)  27.5 us
    dot_general x20, matrix products, cmul(): matmul(lim, rre)  11.3 us
    dot_general x20, matrix products, cmul(): matmul(lim, rim)  11.3 us
    dot_general x20, matrix products, cmul(): matmul(lre, rre) - matmul(lim, rim)  11.3 us
    dot_general x20, matrix products, cmul(): matmul(lre, rim) + matmul(lim, rre)  11.3 us
    select_n x3, other arithmetic, backward_turn(): jnp.where(active, lax.dynamic_update_slice_in_dim(stored, full, pick, 0),...  6.05 us
    add x1, other arithmetic, body(): sigma = sigma + mode_strength[mode] * (lower[:, 0] + upper[:, 0])  5.76 us
  transfers between devices with their start and end apart: 8, of which 6 were waited for; matrix products, arithmetic and copies ran while one was open for 6% of the time, Pallas kernels for 0%

commit v1 on v0

--- a/solution.py
+++ b/solution.py
@@ -3,6 +3,8 @@
 import jax
 import jax.numpy as jnp
 from jax import lax
+from jax.experimental import pallas as pl
+from jax.experimental.pallas import tpu as pltpu
 from jax.sharding import PartitionSpec as P
 
 ETA = 1.0
@@ -132,9 +134,240 @@
     return fulls[:, None]
 
 
+MESH = pl.DeviceIdType.MESH
+CHUNKS = 4
+
+
+def split(value):
+    high = value.astype(jnp.bfloat16)
+    low = (value - high.astype(jnp.float32)).astype(jnp.bfloat16)
+    return high, low
+
+
+def cmul_split(a, b):
+    (arh, arl), (aih, ail) = split(a[0]), split(a[1])
+    (brh, brl), (bih, bil) = split(b[0]), split(b[1])
+    lhs = jnp.concatenate([arh, aih, arl, ail, arh, aih], axis=1)
+    real = jnp.concatenate([brh, -bih, brh, -bih, brl, -bil], axis=0)
+    imag = jnp.concatenate([bih, brh, bih, brh, bil, brl], axis=0)
+    dot = partial(jnp.dot, preferred_element_type=jnp.float32)
+    return dot(lhs, real), dot(lhs, imag)
+
+
+def adj(block):
+    return block[0].T, -block[1].T
+
+
+def wire_kernel(
+    count, strength, shift, green, ham, onsite, hop, out,
+    halo_lo, halo_hi, local, mat, link, site, coup, left,
+    next_send, prev_send, lo_recv, hi_recv, mat_send, mat_recv, small_send, small_recv,
+):
+    me, sec = lax.axis_index("energy"), lax.axis_index("section")
+    norb = green.shape[-1]
+    rows = norb // CHUNKS
+    has_prev, has_next = me > 0, me < count // 2 - 1
+    odd = lax.rem(me, 2)
+    mate = me + 1 - 2 * odd
+    other = 1 - sec
+
+    barrier = pltpu.get_barrier_semaphore()
+    pl.semaphore_signal(barrier, inc=1, device_id=(me, other), device_id_type=MESH)
+
+    @pl.when(has_prev)
+    def _():
+        pl.semaphore_signal(barrier, inc=1, device_id=(me - 1, sec), device_id_type=MESH)
+
+    @pl.when(has_next)
+    def _():
+        pl.semaphore_signal(barrier, inc=1, device_id=(me + 1, sec), device_id_type=MESH)
+
+    pl.semaphore_wait(barrier, 1 + has_prev.astype(jnp.int32) + has_next.astype(jnp.int32))
+
+    def cut(c):
+        return pl.ds(c * rows, rows)
+
+    def to_next(c):
+        return pltpu.make_async_remote_copy(
+            green.at[:, 0, :, cut(c)], halo_lo.at[:, :, cut(c)], next_send.at[c], lo_recv.at[c],
+            device_id=(me + 1, sec), device_id_type=MESH)
+
+    def to_prev(c):
+        return pltpu.make_async_remote_copy(
+            green.at[:, 0, :, cut(c)], halo_hi.at[:, :, cut(c)], prev_send.at[c], hi_recv.at[c],
+            device_id=(me - 1, sec), device_id_type=MESH)
+
+    def swap(c, slab):
+        return pltpu.make_async_remote_copy(
+            mat.at[slab, :, :, cut(c)], mat.at[slab, :, :, cut(c)], mat_send.at[c], mat_recv.at[c],
+            device_id=(me, other), device_id_type=MESH)
+
+    def site_copy(slab):
+        return pltpu.make_async_remote_copy(
+            site.at[slab], site.at[slab], small_send.at[0], small_recv.at[0],
+            device_id=(me, other), device_id_type=MESH)
+
+    def link_down():
+        return pltpu.make_async_remote_copy(
+            hop.at[0, odd], link.at[odd], small_send.at[1], small_recv.at[1],
+            device_id=(me, other), device_id_type=MESH)
+
+    def link_across(part):
+        return pltpu.make_async_remote_copy(
+            link.at[part], link.at[part], small_send.at[2], small_recv.at[2],
+            device_id=(mate, sec), device_id_type=MESH)
+
+    for c in range(CHUNKS):
+        pl.when(has_next)(lambda c=c: to_next(c).start())
+        pl.when(has_prev)(lambda c=c: to_prev(c).start())
+    pl.when(sec == 1)(lambda: link_down().start())
+    site[sec] = jnp.broadcast_to(onsite[...], (8, norb))
+    site_copy(sec).start()
+
+    @pl.when(jnp.logical_not(has_prev))
+    def _():
+        halo_lo[...] = jnp.zeros(halo_lo.shape, jnp.float32)
+
+    @pl.when(jnp.logical_not(has_next))
+    def _():
+        halo_hi[...] = jnp.zeros(halo_hi.shape, jnp.float32)
+
+    eye = lax.broadcasted_iota(jnp.int32, (norb, norb), 0) == lax.broadcasted_iota(
+        jnp.int32, (norb, norb), 1)
+    one = jnp.where(eye, 1.0, 0.0)
+    w1, w2 = jnp.float32(0.0), jnp.float32(0.0)
+    for m in range(strength.shape[0]):
+        w1 = w1 + jnp.where(shift[m] == 1, strength[m], 0.0)
+        w2 = w2 + jnp.where(shift[m] == 2, strength[m], 0.0)
+
+    def energy(k):
+        return -1.5 + 3.0 * ((2 * me + k).astype(jnp.float32) + 0.5) / count
+
+    local[0] = 0.5 * (ham[0, 0] + ham[0, 0].T) + jnp.where(eye, onsite[...], 0.0)
+    local[1] = 0.5 * (ham[0, 1] - ham[0, 1].T) - one * ETA
+
+    @pl.when(sec == 0)
+    def _():
+        block = hop[0, 0], hop[0, 1]
+        real, imag = cmul_split(adj(block), block)
+        local[0] = local[0] + LEAD * imag
+        local[1] = local[1] - LEAD * real
+        link_down().wait_recv()
+        link_across(odd).start()
+
+    @pl.when(sec == 1)
+    def _():
+        link[...] = hop[0]
+
+    for c in range(CHUNKS):
+        pl.when(has_prev)(lambda c=c: to_next(c).wait_recv())
+        pl.when(has_next)(lambda c=c: to_prev(c).wait_recv())
+        r = slice(c * rows, (c + 1) * rows)
+        for part in range(2):
+            here0, here1 = green[0, 0, part, r], green[1, 0, part, r]
+            low0, low1 = halo_lo[0, part, r], halo_lo[1, part, r]
+            high0, high1 = halo_hi[0, part, r], halo_hi[1, part, r]
+            base = local[part, r]
+            first = -base - w1 * (low1 + here1) - w2 * (low0 + high0)
+            second = -base - w1 * (here0 + high0) - w2 * (low1 + high1)
+            if part == 0:
+                first = first + one[r] * energy(0)
+                second = second + one[r] * energy(1)
+            mat[sec, 0, part, r] = first
+            mat[sec, 1, part, r] = second
+        swap(c, sec).start()
+
+    def newton(matrix, slab, k):
+        row = energy(k) - site[slab][:1]
+        col = jnp.sum(jnp.where(eye, row, 0.0), axis=1, keepdims=True)
+        rre = row / (row * row + ETA * ETA)
+        rim = -ETA / (row * row + ETA * ETA)
+        cre = col / (col * col + ETA * ETA)
+        cim = -ETA / (col * col + ETA * ETA)
+        wre, wim = cre * rre - cim * rim, cre * rim + cim * rre
+        xre = jnp.where(eye, 2.0 * rre, 0.0) - (matrix[0] * wre - matrix[1] * wim)
+        xim = jnp.where(eye, 2.0 * rim, 0.0) - (matrix[0] * wim + matrix[1] * wre)
+        guess = xre, xim
+        again = cmul_split(guess, cmul_split(matrix, guess))
+        return 2.0 * xre - again[0], 2.0 * xim - again[1]
+
+    site_copy(other).wait_recv()
+
+    @pl.when(sec == 0)
+    def _():
+        link_across(1 - odd).wait_recv()
+
+    @pl.when(sec == 1)
+    def _():
+        for c in range(CHUNKS):
+            swap(c, 0).wait_recv()
+
+    for k in range(2):
+        g = newton((mat[0, k, 0], mat[0, k, 1]), 0, k)
+        left[k, 0], left[k, 1] = g
+        block = link[0], link[1]
+        coup[k, 0], coup[k, 1] = cmul_split(cmul_split(adj(block), g), block)
+
+    @pl.when(sec == 0)
+    def _():
+        for c in range(CHUNKS):
+            swap(c, 1).wait_recv()
+
+    for k in range(2):
+        g = newton((mat[1, k, 0] - coup[k, 0], mat[1, k, 1] - coup[k, 1]), 1, k)
+        out[k, 0, 0], out[k, 0, 1] = g
+
+        @pl.when(sec == 0)
+        def _(k=k):
+            block = link[0], link[1]
+            g1 = out[k, 0, 0], out[k, 0, 1]
+            g0 = left[k, 0], left[k, 1]
+            right = cmul_split(cmul_split(block, g1), adj(block))
+            more = cmul_split(g0, cmul_split(right, g0))
+            out[k, 0, 0] = g0[0] + more[0]
+            out[k, 0, 1] = g0[1] + more[1]
+
+    for c in range(CHUNKS):
+        pl.when(has_next)(lambda c=c: to_next(c).wait_send())
+        pl.when(has_prev)(lambda c=c: to_prev(c).wait_send())
+        swap(c, sec).wait_send()
+    site_copy(sec).wait_send()
+    pl.when(sec == 1)(lambda: link_down().wait_send())
+    pl.when(sec == 0)(lambda: link_across(odd).wait_send())
+
+
+def two_slabs(green_prev, slab_ham, onsite, hop, mode_strength, phonon_shift):
+    norb = green_prev.shape[3]
+    count = green_prev.shape[0] * lax.axis_size("energy")
+    vmem = pl.BlockSpec(memory_space=pltpu.VMEM)
+    smem = pl.BlockSpec(memory_space=pltpu.SMEM)
+    pair = pltpu.VMEM((2, 2, norb, norb), jnp.float32)
+    sems = pltpu.SemaphoreType.DMA((CHUNKS,))
+    return pl.pallas_call(
+        partial(wire_kernel, count),
+        out_shape=jax.ShapeDtypeStruct(green_prev.shape, jnp.float32),
+        in_specs=[smem, smem, vmem, vmem, vmem, vmem],
+        out_specs=vmem,
+        scratch_shapes=[
+            pair, pair,
+            pltpu.VMEM((2, norb, norb), jnp.float32),
+            pltpu.VMEM((2, 2, 2, norb, norb), jnp.float32),
+            pltpu.VMEM((2, norb, norb), jnp.float32),
+            pltpu.VMEM((2, 8, norb), jnp.float32),
+            pair, pair,
+            sems, sems, sems, sems, sems, sems,
+            pltpu.SemaphoreType.DMA((3,)),
+            pltpu.SemaphoreType.DMA((3,)),
+        ],
+        compiler_params=pltpu.CompilerParams(
+            collective_id=0, has_side_effects=True, vmem_limit_bytes=48 * 1024 * 1024),
+        name="wire",
+    )(mode_strength, phonon_shift, green_prev, slab_ham, onsite, hop)
+
+
 def solution(mesh):
     return jax.shard_map(
-        body,
+        two_slabs if mesh.shape["section"] == 2 and mesh.shape["energy"] % 2 == 0 else body,
         mesh=mesh,
         in_specs=(
             P("energy", "section", None, None, None),

time: 204 us -> 48.6 us (0.24)
  the two profiles are of different devices: /device:TPU:0 before, /device:TPU:19 now
where the time goes in v1:
time: 48.6 us; the launch traced here: 48.3 us
  Pallas kernels  42 us (86%)
  local copies, waits for them, and re-layouts  6.27 us (13%)
    pallas_call x1, Pallas kernels, two_slabs(): pl.pallas_call(partial(wire_kernel, count), out_shape=jax.ShapeDtypeStruc...  42 us
    unnamed x13, local copies, waits for them, and re-layouts  6.27 us

profile of v1, /device:TPU:19, one launch (start us, length us, event | category | flops | bytes accessed | tf_op | source)
XLA Modules:
  0.0 48.3 jit_solution(14687962728556245043)
XLA Ops:
  0.0 0.0 copy-start
  0.0 1.2 %copy-done = f32[2,1,2,256,256]{4,3,2,1,0:T(8,128)S(1)} copy-done((f32[2,1,2,256,256]{4,3,2,1,0:T(8,128)S(1)}, f32[2,1,2,256,256]{4,3,2,1,0:T(8,128)}, u32[]{:S(2)}) %copy-start) | copy-done | bytes 1048600
  1.2 0.0 copy-start.1
  1.2 1.0 %copy-done.1 = f32[1,2,256,256]{3,2,1,0:T(8,128)S(1)} copy-done((f32[1,2,256,256]{3,2,1,0:T(8,128)S(1)}, f32[1,2,256,256]{3,2,1,0:T(8,128)}, u32[]{:S(2)}) %copy-start.1) | copy-done | bytes 524312
  2.3 0.0 copy-start.2
  2.3 1.0 %copy-done.2 = f32[1,2,256,256]{3,2,1,0:T(8,128)S(1)} copy-done((f32[1,2,256,256]{3,2,1,0:T(8,128)S(1)}, f32[1,2,256,256]{3,2,1,0:T(8,128)}, u32[]{:S(2)}) %copy-start.2) | copy-done | bytes 524312
  3.3 0.0 copy-start.3
  3.3 0.7 %copy-done.3 = f32[1,256]{1,0:T(1,128)S(1)} copy-done((f32[1,256]{1,0:T(1,128)S(1)}, f32[1,256]{1,0:T(1,128)}, u32[]{:S(2)}) %copy-start.3) | copy-done | bytes 1048
  4.0 0.0 copy-start.4
  4.0 0.7 %copy-done.4 = f32[6]{0:T(128)S(1)} copy-done((f32[6]{0:T(128)S(1)}, f32[6]{0:T(128)}, u32[]{:S(2)}) %copy-start.4) | copy-done | bytes 48
  4.6 0.0 copy-start.5
  4.6 0.7 %copy-done.5 = s32[6]{0:T(128)S(1)} copy-done((s32[6]{0:T(128)S(1)}, s32[6]{0:T(128)}, u32[]{:S(2)}) %copy-start.5) | copy-done | bytes 48
  5.3 42.0 %wire.1 = f32[2,1,2,256,256]{4,3,2,1,0:T(8,128)S(1)} custom-call(f32[6]{0:T(128)S(1)} %copy-done.4, s32[6]{0:T(128)S(1)} %copy-done.5, f32[2,1,2,256,256]{4,3,2,1,0:T(8,128)S(1)} %copy-done, f32[1,2,256,256]{3,2,1,0:T(8,128)S(1)} %copy-done.1, f32[1,256]{1,0:T(1,128)S(1)} %copy-done.3, f32[1,2,256,256]{3,2,1,0:T(8,128)S(1)} %copy-done.2), custom_call_target="tpu_custom_call" | custom-call | tf_op jit(solution)/shard_map/wire/pallas_call | solution.py:346
  47.3 1.0 %copy.8 = f32[2,1,2,256,256]{4,3,2,1,0:T(8,128)} copy(f32[2,1,2,256,256]{4,3,2,1,0:T(8,128)S(1)} %wire.1) | data formatting | bytes 2097152
Async XLA Ops:
  0.0 1.2 %copy-start = (f32[2,1,2,256,256]{4,3,2,1,0:T(8,128)S(1)}, f32[2,1,2,256,256]{4,3,2,1,0:T(8,128)}, u32[]{:S(2)}) copy-start(f32[2,1,2,256,256]{4,3,2,1,0:T(8,128)} %green.1) | copy-start | bytes 3145732
  1.2 1.0 %copy-start.1 = (f32[1,2,256,256]{3,2,1,0:T(8,128)S(1)}, f32[1,2,256,256]{3,2,1,0:T(8,128)}, u32[]{:S(2)}) copy-start(f32[1,2,256,256]{3,2,1,0:T(8,128)} %ham.1) | copy-start | bytes 1572868
  2.3 1.0 %copy-start.2 = (f32[1,2,256,256]{3,2,1,0:T(8,128)S(1)}, f32[1,2,256,256]{3,2,1,0:T(8,128)}, u32[]{:S(2)}) copy-start(f32[1,2,256,256]{3,2,1,0:T(8,128)} %hop.1) | copy-start | bytes 1572868
  3.3 0.7 %copy-start.3 = (f32[1,256]{1,0:T(1,128)S(1)}, f32[1,256]{1,0:T(1,128)}, u32[]{:S(2)}) copy-start(f32[1,256]{1,0:T(1,128)} %onsite.1) | copy-start | bytes 3076
  4.0 0.7 %copy-start.4 = (f32[6]{0:T(128)S(1)}, f32[6]{0:T(128)}, u32[]{:S(2)}) copy-start(f32[6]{0:T(128)} %strength.1) | copy-start | bytes 76
  4.6 0.7 %copy-start.5 = (s32[6]{0:T(128)S(1)}, s32[6]{0:T(128)}, u32[]{:S(2)}) copy-start(s32[6]{0:T(128)} %shift.1) | copy-start | bytes 76

commit v2 on v1

--- a/solution.py
+++ b/solution.py
@@ -159,48 +159,61 @@
 
 
 def wire_kernel(
-    count, strength, shift, green, ham, onsite, hop, out,
-    halo_lo, halo_hi, local, mat, link, site, coup, left,
-    next_send, prev_send, lo_recv, hi_recv, mat_send, mat_recv, small_send, small_recv,
+    count, strength_hbm, shift_hbm, green_hbm, ham_hbm, onsite_hbm, hop_hbm, out_hbm,
+    strength, shift, green, ham, onsite, hop, far_buf, mate_buf, local, mat, link, link_h, site,
+    coup, left, result,
+    load_sem, far_send, far_recv, mate_send, mate_recv, mat_send, mat_recv, small_send, small_recv,
+    out_sem,
 ):
     me, sec = lax.axis_index("energy"), lax.axis_index("section")
     norb = green.shape[-1]
     rows = norb // CHUNKS
-    has_prev, has_next = me > 0, me < count // 2 - 1
     odd = lax.rem(me, 2)
-    mate = me + 1 - 2 * odd
+    mate, far = me + 1 - 2 * odd, me - 1 + 2 * odd
+    has_far = jnp.logical_and(far >= 0, far < count // 2)
     other = 1 - sec
+    order = (1 - odd, odd)
+
+    loads = [
+        pltpu.make_async_copy(source, target, load_sem.at[n])
+        for n, (source, target) in enumerate((
+            (strength_hbm, strength), (shift_hbm, shift), (onsite_hbm, onsite),
+            (hop_hbm.at[0], hop), (ham_hbm.at[0], ham), (green_hbm.at[:, 0], green)))
+    ]
+    for load in loads:
+        load.start()
 
     barrier = pltpu.get_barrier_semaphore()
     pl.semaphore_signal(barrier, inc=1, device_id=(me, other), device_id_type=MESH)
-
-    @pl.when(has_prev)
-    def _():
-        pl.semaphore_signal(barrier, inc=1, device_id=(me - 1, sec), device_id_type=MESH)
-
-    @pl.when(has_next)
-    def _():
-        pl.semaphore_signal(barrier, inc=1, device_id=(me + 1, sec), device_id_type=MESH)
-
-    pl.semaphore_wait(barrier, 1 + has_prev.astype(jnp.int32) + has_next.astype(jnp.int32))
+    pl.semaphore_signal(barrier, inc=1, device_id=(mate, sec), device_id_type=MESH)
+
+    @pl.when(has_far)
+    def _():
+        pl.semaphore_signal(barrier, inc=1, device_id=(far, sec), device_id_type=MESH)
+
+    pl.semaphore_wait(barrier, 2 + has_far.astype(jnp.int32))
 
     def cut(c):
         return pl.ds(c * rows, rows)
 
-    def to_next(c):
-        return pltpu.make_async_remote_copy(
-            green.at[:, 0, :, cut(c)], halo_lo.at[:, :, cut(c)], next_send.at[c], lo_recv.at[c],
-            device_id=(me + 1, sec), device_id_type=MESH)
-
-    def to_prev(c):
-        return pltpu.make_async_remote_copy(
-            green.at[:, 0, :, cut(c)], halo_hi.at[:, :, cut(c)], prev_send.at[c], hi_recv.at[c],
-            device_id=(me - 1, sec), device_id_type=MESH)
-
-    def swap(c, slab):
-        return pltpu.make_async_remote_copy(
-            mat.at[slab, :, :, cut(c)], mat.at[slab, :, :, cut(c)], mat_send.at[c], mat_recv.at[c],
-            device_id=(me, other), device_id_type=MESH)
+    def to_far(j, c):
+        source = odd if j == 0 else 1 - odd
+        n = j * CHUNKS + c
+        return pltpu.make_async_remote_copy(
+            green_hbm.at[source, 0, :, cut(c)], far_buf.at[j, :, cut(c)], far_send.at[n],
+            far_recv.at[n], device_id=(far, sec), device_id_type=MESH)
+
+    def to_mate(j):
+        source = 1 - odd if j == 0 else odd
+        return pltpu.make_async_remote_copy(
+            green_hbm.at[source, 0], mate_buf.at[j], mate_send.at[j], mate_recv.at[j],
+            device_id=(mate, sec), device_id_type=MESH)
+
+    def swap(j, c, slab):
+        n = j * CHUNKS + c
+        return pltpu.make_async_remote_copy(
+            mat.at[slab, j, :, cut(c)], mat.at[slab, j, :, cut(c)], mat_send.at[n],
+            mat_recv.at[n], device_id=(me, other), device_id_type=MESH)
 
     def site_copy(slab):
         return pltpu.make_async_remote_copy(
@@ -209,7 +222,7 @@
 
     def link_down():
         return pltpu.make_async_remote_copy(
-            hop.at[0, odd], link.at[odd], small_send.at[1], small_recv.at[1],
+            hop_hbm.at[0, odd], link.at[odd], small_send.at[1], small_recv.at[1],
             device_id=(me, other), device_id_type=MESH)
 
     def link_across(part):
@@ -217,24 +230,31 @@
             link.at[part], link.at[part], small_send.at[2], small_recv.at[2],
             device_id=(mate, sec), device_id_type=MESH)
 
-    for c in range(CHUNKS):
-        pl.when(has_next)(lambda c=c: to_next(c).start())
-        pl.when(has_prev)(lambda c=c: to_prev(c).start())
+    @pl.when(has_far)
+    def _():
+        for c in range(CHUNKS):
+            to_far(0, c).start()
+
+    to_mate(0).start()
+    to_mate(1).start()
     pl.when(sec == 1)(lambda: link_down().start())
+
+    @pl.when(has_far)
+    def _():
+        for c in range(CHUNKS):
+            to_far(1, c).start()
+
+    @pl.when(jnp.logical_not(has_far))
+    def _():
+        far_buf[...] = jnp.zeros(far_buf.shape, jnp.float32)
+
+    for load in loads:
+        load.wait()
     site[sec] = jnp.broadcast_to(onsite[...], (8, norb))
     site_copy(sec).start()
 
-    @pl.when(jnp.logical_not(has_prev))
-    def _():
-        halo_lo[...] = jnp.zeros(halo_lo.shape, jnp.float32)
-
-    @pl.when(jnp.logical_not(has_next))
-    def _():
-        halo_hi[...] = jnp.zeros(halo_hi.shape, jnp.float32)
-
     eye = lax.broadcasted_iota(jnp.int32, (norb, norb), 0) == lax.broadcasted_iota(
         jnp.int32, (norb, norb), 1)
-    one = jnp.where(eye, 1.0, 0.0)
     w1, w2 = jnp.float32(0.0), jnp.float32(0.0)
     for m in range(strength.shape[0]):
         w1 = w1 + jnp.where(shift[m] == 1, strength[m], 0.0)
@@ -243,12 +263,12 @@
     def energy(k):
         return -1.5 + 3.0 * ((2 * me + k).astype(jnp.float32) + 0.5) / count
 
-    local[0] = 0.5 * (ham[0, 0] + ham[0, 0].T) + jnp.where(eye, onsite[...], 0.0)
-    local[1] = 0.5 * (ham[0, 1] - ham[0, 1].T) - one * ETA
+    local[0] = 0.5 * (ham[0] + ham[0].T) + jnp.where(eye, onsite[...], 0.0)
+    local[1] = 0.5 * (ham[1] - ham[1].T) - jnp.where(eye, ETA, 0.0)
 
     @pl.when(sec == 0)
     def _():
-        block = hop[0, 0], hop[0, 1]
+        block = hop[0], hop[1]
         real, imag = cmul_split(adj(block), block)
         local[0] = local[0] + LEAD * imag
         local[1] = local[1] - LEAD * real
@@ -257,25 +277,26 @@
 
     @pl.when(sec == 1)
     def _():
-        link[...] = hop[0]
-
-    for c in range(CHUNKS):
-        pl.when(has_prev)(lambda c=c: to_next(c).wait_recv())
-        pl.when(has_next)(lambda c=c: to_prev(c).wait_recv())
+        link[...] = hop[...]
+        link_h[0], link_h[1] = adj((hop[0], hop[1]))
+
+    to_mate(0).wait_recv()
+    to_mate(1).wait_recv()
+
+    def assemble(j, c):
+        pl.when(has_far)(lambda: to_far(j, c).wait_recv())
         r = slice(c * rows, (c + 1) * rows)
         for part in range(2):
-            here0, here1 = green[0, 0, part, r], green[1, 0, part, r]
-            low0, low1 = halo_lo[0, part, r], halo_lo[1, part, r]
-            high0, high1 = halo_hi[0, part, r], halo_hi[1, part, r]
-            base = local[part, r]
-            first = -base - w1 * (low1 + here1) - w2 * (low0 + high0)
-            second = -base - w1 * (here0 + high0) - w2 * (low1 + high1)
+            near, here = far_buf[0, part, r], green[1 - order[j], part, r]
+            if j == 0:
+                sigma = w1 * (here + mate_buf[0, part, r]) + w2 * (near + mate_buf[1, part, r])
+            else:
+                sigma = w1 * (here + near) + w2 * (far_buf[1, part, r] + mate_buf[0, part, r])
+            value = -local[part, r] - sigma
             if part == 0:
-                first = first + one[r] * energy(0)
-                second = second + one[r] * energy(1)
-            mat[sec, 0, part, r] = first
-            mat[sec, 1, part, r] = second
-        swap(c, sec).start()
+                value = value + jnp.where(eye[r], energy(order[j]), 0.0)
+            mat[sec, j, part, r] = value
+        swap(j, c, sec).start()
 
     def newton(matrix, slab, k):
         row = energy(k) - site[slab][:1]
@@ -291,46 +312,68 @@
         again = cmul_split(guess, cmul_split(matrix, guess))
         return 2.0 * xre - again[0], 2.0 * xim - again[1]
 
-    site_copy(other).wait_recv()
+    def arrived(j, slab):
+        for c in range(CHUNKS):
+            swap(j, c, slab).wait_recv()
+
+    def first_slab(j):
+        g = newton((mat[0, j, 0], mat[0, j, 1]), 0, order[j])
+        left[0], left[1] = g
+        half = cmul_split((link_h[0], link_h[1]), g)
+        coup[0], coup[1] = cmul_split(half, (link[0], link[1]))
+
+    def store(j):
+        return pltpu.make_async_copy(result.at[j], out_hbm.at[order[j], 0], out_sem.at[j])
+
+    def second_slab(j):
+        pl.when(sec == 0)(lambda: arrived(j, 1))
+        g1 = newton((mat[1, j, 0] - coup[0], mat[1, j, 1] - coup[1]), 1, order[j])
+        result[j, 0], result[j, 1] = g1
+
+        @pl.when(sec == 0)
+        def _():
+            g1 = result[j, 0], result[j, 1]
+            g0 = left[0], left[1]
+            half = cmul_split((link[0], link[1]), g1)
+            right = cmul_split(half, (link_h[0], link_h[1]))
+            more = cmul_split(g0, cmul_split(right, g0))
+            result[j, 0] = g0[0] + more[0]
+            result[j, 1] = g0[1] + more[1]
+
+        store(j).start()
+
+    for c in range(CHUNKS):
+        assemble(0, c)
 
     @pl.when(sec == 0)
     def _():
+        site_copy(1).wait_recv()
         link_across(1 - odd).wait_recv()
+        link_h[0], link_h[1] = adj((link[0], link[1]))
+        first_slab(0)
+
+    for c in range(CHUNKS // 2):
+        assemble(1, c)
 
     @pl.when(sec == 1)
     def _():
+        site_copy(0).wait_recv()
+        arrived(0, 0)
+        first_slab(0)
+
+    second_slab(0)
+    for c in range(CHUNKS // 2, CHUNKS):
+        assemble(1, c)
+    pl.when(sec == 1)(lambda: arrived(1, 0))
+    first_slab(1)
+    second_slab(1)
+
+    for j in range(2):
         for c in range(CHUNKS):
-            swap(c, 0).wait_recv()
-
-    for k in range(2):
-        g = newton((mat[0, k, 0], mat[0, k, 1]), 0, k)
-        left[k, 0], left[k, 1] = g
-        block = link[0], link[1]
-        coup[k, 0], coup[k, 1] = cmul_split(cmul_split(adj(block), g), block)
-
-    @pl.when(sec == 0)
-    def _():
-        for c in range(CHUNKS):
-            swap(c, 1).wait_recv()
-
-    for k in range(2):
-        g = newton((mat[1, k, 0] - coup[k, 0], mat[1, k, 1] - coup[k, 1]), 1, k)
-        out[k, 0, 0], out[k, 0, 1] = g
-
-        @pl.when(sec == 0)
-        def _(k=k):
-            block = link[0], link[1]
-            g1 = out[k, 0, 0], out[k, 0, 1]
-            g0 = left[k, 0], left[k, 1]
-            right = cmul_split(cmul_split(block, g1), adj(block))
-            more = cmul_split(g0, cmul_split(right, g0))
-            out[k, 0, 0] = g0[0] + more[0]
-            out[k, 0, 1] = g0[1] + more[1]
-
-    for c in range(CHUNKS):
-        pl.when(has_next)(lambda c=c: to_next(c).wait_send())
-        pl.when(has_prev)(lambda c=c: to_prev(c).wait_send())
-        swap(c, sec).wait_send()
+            pl.when(has_far)(lambda j=j, c=c: to_far(j, c).wait_send())
+            swap(j, c, sec).wait_send()
+        to_mate(j).wait_send()
+        store(j).wait()
     site_copy(sec).wait_send()
     pl.when(sec == 1)(lambda: link_down().wait_send())
     pl.when(sec == 0)(lambda: link_across(odd).wait_send())
@@ -339,28 +382,29 @@
 def two_slabs(green_prev, slab_ham, onsite, hop, mode_strength, phonon_shift):
     norb = green_prev.shape[3]
     count = green_prev.shape[0] * lax.axis_size("energy")
-    vmem = pl.BlockSpec(memory_space=pltpu.VMEM)
-    smem = pl.BlockSpec(memory_space=pltpu.SMEM)
+    hbm = pl.BlockSpec(memory_space=pltpu.HBM)
+    one = pltpu.VMEM((2, norb, norb), jnp.float32)
     pair = pltpu.VMEM((2, 2, norb, norb), jnp.float32)
-    sems = pltpu.SemaphoreType.DMA((CHUNKS,))
+    sems = lambda n: pltpu.SemaphoreType.DMA((n,))
     return pl.pallas_call(
         partial(wire_kernel, count),
         out_shape=jax.ShapeDtypeStruct(green_prev.shape, jnp.float32),
-        in_specs=[smem, smem, vmem, vmem, vmem, vmem],
-        out_specs=vmem,
+        in_specs=[hbm] * 6,
+        out_specs=hbm,
         scratch_shapes=[
-            pair, pair,
-            pltpu.VMEM((2, norb, norb), jnp.float32),
+            pltpu.SMEM(mode_strength.shape, jnp.float32),
+            pltpu.SMEM(phonon_shift.shape, jnp.int32),
+            pair, one, pltpu.VMEM(onsite.shape, jnp.float32), one,
+            pair, pair, one,
             pltpu.VMEM((2, 2, 2, norb, norb), jnp.float32),
-            pltpu.VMEM((2, norb, norb), jnp.float32),
+            one, one,
             pltpu.VMEM((2, 8, norb), jnp.float32),
-            pair, pair,
-            sems, sems, sems, sems, sems, sems,
-            pltpu.SemaphoreType.DMA((3,)),
-            pltpu.SemaphoreType.DMA((3,)),
+            one, one, pair,
+            sems(6), sems(2 * CHUNKS), sems(2 * CHUNKS), sems(2), sems(2),
+            sems(2 * CHUNKS), sems(2 * CHUNKS), sems(3), sems(3), sems(2),
         ],
         compiler_params=pltpu.CompilerParams(
-            collective_id=0, has_side_effects=True, vmem_limit_bytes=48 * 1024 * 1024),
+            collective_id=0, has_side_effects=True, vmem_limit_bytes=63 * 1024 * 1024),
         name="wire",
     )(mode_strength, phonon_shift, green_prev, slab_ham, onsite, hop)
 

time: 48.6 us -> 44.5 us (0.916)
  the two profiles are of different devices: /device:TPU:19 before, /device:TPU:20 now
where the time goes in v2:
time: 44.5 us; the launch traced here: 44.4 us
  Pallas kernels  42.1 us (95%)
  local copies, waits for them, and re-layouts  2.29 us (5%)
    pallas_call x1, Pallas kernels, two_slabs(): pl.pallas_call(partial(wire_kernel, count), out_shape=jax.ShapeDtypeStruc...  42.1 us
    unnamed x1, local copies, waits for them, and re-layouts  2.29 us

profile of v2, /device:TPU:20, one launch (start us, length us, event | category | flops | bytes accessed | tf_op | source)
XLA Modules:
  0.0 44.4 jit_solution(10772060822223275212)
XLA Ops:
  0.0 42.1 %wire.1 = f32[2,1,2,256,256]{4,3,2,1,0:T(8,128)} custom-call(f32[6]{0:T(128)} %strength_hbm.1, s32[6]{0:T(128)} %shift_hbm.1, f32[2,1,2,256,256]{4,3,2,1,0:T(8,128)} %green_hbm.1, f32[1,2,256,256]{3,2,1,0:T(8,128)} %ham_hbm.1, f32[1,256]{1,0:T(1,128)} %onsite_hbm.1, f32[1,2,256,256]{3,2,1,0:T(8,128)} %hop_hbm.1), custom_call_target="tpu_custom_call" | custom-call | tf_op jit(solution)/shard_map/wire/pallas_call | solution.py:389
  42.1 2.3 %copy.8 = f32[2,1,2,256,256]{4,3,2,1,0:T(8,128)} copy(f32[2,1,2,256,256]{4,3,2,1,0:T(8,128)} %wire.1) | data formatting | bytes 2097152

commit v3 on v2

--- a/solution.py
+++ b/solution.py
@@ -144,14 +144,18 @@
     return high, low
 
 
+def product(a, b):
+    (ah, al), (bh, bl) = a, b
+    return jnp.dot(
+        jnp.concatenate([ah, al, ah], axis=1), jnp.concatenate([bh, bh, bl], axis=0),
+        preferred_element_type=jnp.float32)
+
+
 def cmul_split(a, b):
-    (arh, arl), (aih, ail) = split(a[0]), split(a[1])
-    (brh, brl), (bih, bil) = split(b[0]), split(b[1])
-    lhs = jnp.concatenate([arh, aih, arl, ail, arh, aih], axis=1)
-    real = jnp.concatenate([brh, -bih, brh, -bih, brl, -bil], axis=0)
-    imag = jnp.concatenate([bih, brh, bih, brh, bil, brl], axis=0)
-    dot = partial(jnp.dot, preferred_element_type=jnp.float32)
-    return dot(lhs, real), dot(lhs, imag)
+    rere = product(split(a[0]), split(b[0]))
+    imim = product(split(a[1]), split(b[1]))
+    mixed = product(split(a[0] + a[1]), split(b[0] + b[1]))
+    return rere - imim, mixed - rere - imim
 
 
 def adj(block):
@@ -230,6 +234,8 @@
             link.at[part], link.at[part], small_send.at[2], small_recv.at[2],
             device_id=(mate, sec), device_id_type=MESH)
 
+    pl.when(sec == 1)(lambda: link_down().start())
+
     @pl.when(has_far)
     def _():
         for c in range(CHUNKS):
@@ -237,7 +243,6 @@
 
     to_mate(0).start()
     to_mate(1).start()
-    pl.when(sec == 1)(lambda: link_down().start())
 
     @pl.when(has_far)
     def _():
@@ -272,8 +277,6 @@
         real, imag = cmul_split(adj(block), block)
         local[0] = local[0] + LEAD * imag
         local[1] = local[1] - LEAD * real
-        link_down().wait_recv()
-        link_across(odd).start()
 
     @pl.when(sec == 1)
     def _():
@@ -319,7 +322,9 @@
     def first_slab(j):
         g = newton((mat[0, j, 0], mat[0, j, 1]), 0, order[j])
         left[0], left[1] = g
-        half = cmul_split((link_h[0], link_h[1]), g)
+
+    def couple():
+        half = cmul_split((link_h[0], link_h[1]), (left[0], left[1]))
         coup[0], coup[1] = cmul_split(half, (link[0], link[1]))
 
     def store(j):
@@ -347,13 +352,17 @@
 
     @pl.when(sec == 0)
     def _():
+        link_down().wait_recv()
+        link_across(odd).start()
         site_copy(1).wait_recv()
+        first_slab(0)
+
+    assemble(1, 0)
+
+    @pl.when(sec == 0)
+    def _():
         link_across(1 - odd).wait_recv()
         link_h[0], link_h[1] = adj((link[0], link[1]))
-        first_slab(0)
-
-    for c in range(CHUNKS // 2):
-        assemble(1, c)
 
     @pl.when(sec == 1)
     def _():
@@ -361,11 +370,14 @@
         arrived(0, 0)
         first_slab(0)
 
+    couple()
+    for c in range(1, CHUNKS - 1):
+        assemble(1, c)
     second_slab(0)
-    for c in range(CHUNKS // 2, CHUNKS):
-        assemble(1, c)
+    assemble(1, CHUNKS - 1)
     pl.when(sec == 1)(lambda: arrived(1, 0))
     first_slab(1)
+    couple()
     second_slab(1)
 
     for j in range(2):

time: 44.5 us -> 41.5 us (0.933)
  the two profiles are of different devices: /device:TPU:20 before, /device:TPU:22 now
where the time goes in v3:
time: 41.5 us; the launch traced here: 41.3 us
  Pallas kernels  39 us (94%)
  local copies, waits for them, and re-layouts  2.29 us (6%)
    pallas_call x1, Pallas kernels, two_slabs(): pl.pallas_call(partial(wire_kernel, count), out_shape=jax.ShapeDtypeStruc...  39 us
    unnamed x1, local copies, waits for them, and re-layouts  2.29 us

profile of v3, /device:TPU:22, one launch (start us, length us, event | category | flops | bytes accessed | tf_op | source)
XLA Modules:
  0.0 41.3 jit_solution(4003730790390735724)
XLA Ops:
  0.0 39.0 %wire.1 = f32[2,1,2,256,256]{4,3,2,1,0:T(8,128)} custom-call(f32[6]{0:T(128)} %strength_hbm.1, s32[6]{0:T(128)} %shift_hbm.1, f32[2,1,2,256,256]{4,3,2,1,0:T(8,128)} %green_hbm.1, f32[1,2,256,256]{3,2,1,0:T(8,128)} %ham_hbm.1, f32[1,256]{1,0:T(1,128)} %onsite_hbm.1, f32[1,2,256,256]{3,2,1,0:T(8,128)} %hop_hbm.1), custom_call_target="tpu_custom_call" | custom-call | tf_op jit(solution)/shard_map/wire/pallas_call | solution.py:401
  39.0 2.3 %copy.8 = f32[2,1,2,256,256]{4,3,2,1,0:T(8,128)} copy(f32[2,1,2,256,256]{4,3,2,1,0:T(8,128)} %wire.1) | data formatting | bytes 2097152

commit v4 on v3

--- a/solution.py
+++ b/solution.py
@@ -135,7 +135,7 @@
 
 
 MESH = pl.DeviceIdType.MESH
-CHUNKS = 4
+CHUNKS = 8
 
 
 def split(value):
@@ -357,7 +357,8 @@
         site_copy(1).wait_recv()
         first_slab(0)
 
-    assemble(1, 0)
+    for c in range(CHUNKS // 4):
+        assemble(1, c)
 
     @pl.when(sec == 0)
     def _():
@@ -371,10 +372,11 @@
         first_slab(0)
 
     couple()
-    for c in range(1, CHUNKS - 1):
+    for c in range(CHUNKS // 4, CHUNKS * 3 // 4):
         assemble(1, c)
     second_slab(0)
-    assemble(1, CHUNKS - 1)
+    for c in range(CHUNKS * 3 // 4, CHUNKS):
+        assemble(1, c)
     pl.when(sec == 1)(lambda: arrived(1, 0))
     first_slab(1)
     couple()

time: 41.5 us -> 40.7 us (0.981)
  the two profiles are of different devices: /device:TPU:22 before, /device:TPU:19 now
where the time goes in v4:
time: 40.7 us; the launch traced here: 40.6 us
  Pallas kernels  38.3 us (94%)
  local copies, waits for them, and re-layouts  2.29 us (6%)
    pallas_call x1, Pallas kernels, two_slabs(): pl.pallas_call(partial(wire_kernel, count), out_shape=jax.ShapeDtypeStruc...  38.3 us
    unnamed x1, local copies, waits for them, and re-layouts  2.29 us

profile of v4, /device:TPU:19, one launch (start us, length us, event | category | flops | bytes accessed | tf_op | source)
XLA Modules:
  0.0 40.6 jit_solution(8536930729218580481)
XLA Ops:
  0.0 38.3 %wire.1 = f32[2,1,2,256,256]{4,3,2,1,0:T(8,128)} custom-call(f32[6]{0:T(128)} %strength_hbm.1, s32[6]{0:T(128)} %shift_hbm.1, f32[2,1,2,256,256]{4,3,2,1,0:T(8,128)} %green_hbm.1, f32[1,2,256,256]{3,2,1,0:T(8,128)} %ham_hbm.1, f32[1,256]{1,0:T(1,128)} %onsite_hbm.1, f32[1,2,256,256]{3,2,1,0:T(8,128)} %hop_hbm.1), custom_call_target="tpu_custom_call" | custom-call | tf_op jit(solution)/shard_map/wire/pallas_call | solution.py:403
  38.3 2.3 %copy.8 = f32[2,1,2,256,256]{4,3,2,1,0:T(8,128)} copy(f32[2,1,2,256,256]{4,3,2,1,0:T(8,128)} %wire.1) | data formatting | bytes 2097152
